TPU v7x, 1024 devices: a whole 4x4x32 slice. The times are simulated.
1024 devices in a mesh: blk: 256 (over y, z, x_lo), rep: 4 (over x_hi, core).
Axes of the slice: x: 4 (x_hi: 2, x_lo: 2; x = x_hi * 2 + x_lo), y: 4, z: 32, core: 2. Of those that a mesh axis runs over, the one named last changes fastest.
Arguments:
- features: bfloat16 [131072, 256], P('blk'), may hold values from -6 to 6
- tile_vals: bfloat16 [1024, 64, 128, 128], P('blk', None, 'rep'), may hold values from -0.0625 to 0.0625
- tile_cols: int32 [1024, 64], P('blk'), may hold values from 0 to 1023, as said below
- tile_count: int32 [1024], P('blk'), may hold values from 16 to 64, as said below
- weight: bfloat16 [256, 256], replicated, may hold values from -0.375 to 0.375
- bias: float32 [256], replicated, may hold values from -3 to 3
- cotangent: bfloat16 [131072, 256], P(('blk', 'rep')), may hold values from -6 to 6
Outputs:
- activated: bfloat16 [131072, 256], P(('blk', 'rep'))
- weight_grad: float32 [256, 256], replicated
- bias_grad: float32 [256], replicated
Inputs may be any that keep to these rules, and one draw needn't show every extreme that they name: Entries of one row of tile_cols are distinct; slot 0 of row block i holds i; for every column block j of row block i, j // 4 and i // 4 differ by at most 16, counted cyclically modulo 1024 // 4, and every row block has a column block at that distance on each side. `tile_count`: some row block uses all 64 slots.
All inputs are finite; a program needn't handle non-finite values.
Results may differ from a plain program's by a relative error of at most 0.007.
Values may be sent and summed in bfloat16 or wider, within the bound.
A program may use at most 32 MiB of HBM per device.

v0:
```python
import jax
import jax.numpy as jnp
from jax import lax
from jax.sharding import PartitionSpec as P


def from_behind(x, axis, by):
    length = lax.axis_size(axis)
    return lax.ppermute(x, axis, [(i, (i + by) % length) for i in range(length)])


def body(features, tile_vals, tile_cols, tile_count, weight, bias, cotangent):
    rows_dev = cotangent.shape[0]
    width = features.shape[1]
    blk_dev = tile_cols.shape[0]
    slots = tile_cols.shape[1]
    part_rows = tile_vals.shape[2]
    tile = tile_vals.shape[3]
    n_blk = lax.axis_size("blk")
    reach = n_blk // 16
    own = features.reshape(blk_dev, tile, width)
    share = lax.dynamic_slice_in_dim(own, lax.axis_index("rep") * part_rows, part_rows, 1)
    window = jnp.zeros((2 * reach + 1, blk_dev, part_rows, width), jnp.bfloat16)
    window = lax.dynamic_update_slice_in_dim(window, share[None], reach, 0)

    def turn(step, carry):
        below, above, window = carry
        below = from_behind(below, "blk", 1)
        above = from_behind(above, "blk", -1)
        window = lax.dynamic_update_slice_in_dim(window, below[None], reach - step, 0)
        window = lax.dynamic_update_slice_in_dim(window, above[None], reach + step, 0)
        return (below, above, window)

    below, above, window = lax.fori_loop(1, reach + 1, turn, (share, share, window))
    group = tile_cols // blk_dev
    distance = jnp.mod(group - lax.axis_index("blk") + reach, n_blk)
    flat = distance * blk_dev + tile_cols % blk_dev
    picked = window.reshape((2 * reach + 1) * blk_dev, part_rows, width)[flat]
    valid = jnp.arange(slots, dtype=jnp.int32)[None, :] < tile_count[:, None]
    masked = jnp.where(valid[:, :, None, None], tile_vals, jnp.zeros_like(tile_vals))
    partial_sum = jnp.einsum("isca,iscf->iaf", masked, picked, preferred_element_type=jnp.float32)
    partial_sum = partial_sum.reshape(blk_dev * tile, width)
    totals = lax.psum(partial_sum, "rep")
    summed = lax.dynamic_slice_in_dim(totals, lax.axis_index("rep") * rows_dev, rows_dev, 0)
    aggregated = summed.astype(jnp.bfloat16)
    pre = jnp.dot(aggregated, weight, preferred_element_type=jnp.float32) + bias
    activated = jax.nn.silu(pre).astype(jnp.bfloat16)
    sig = jax.nn.sigmoid(pre)
    grad_pre = (cotangent.astype(jnp.float32) * sig * (1.0 + pre * (1.0 - sig))).astype(
        jnp.bfloat16
    )
    local_weight = lax.dot_general(
        aggregated, grad_pre, (((0,), (0,)), ((), ())), preferred_element_type=jnp.float32
    )
    local_bias = jnp.sum(grad_pre.astype(jnp.float32), axis=0)
    weight_total, bias_total = lax.psum((local_weight, local_bias), ("blk", "rep"))
    node_total = lax.axis_size("blk") * lax.axis_size("rep") * rows_dev
    scale = 1.0 / jnp.sqrt(jnp.float32(node_total))
    return (activated, weight_total * scale, bias_total * scale)


def solution(mesh):
    return jax.shard_map(
        body,
        mesh=mesh,
        in_specs=(
            P("blk", None),
            P("blk", None, "rep", None),
            P("blk", None),
            P("blk"),
            P(),
            P(),
            P(("blk", "rep"), None),
        ),
        out_specs=(P(("blk", "rep"), None), P(), P()),
        check_vma=False,
    )
```

profile of v0, /device:TPU:1, one launch (start us, length us, event | category | flops | bytes accessed | tf_op | source)
XLA Modules:
  0.0 1109.6 jit_solution(14713407088115370830)
XLA Ops:
  9.9 194.9 %while.17 = (s32[]{:T(128)}, bf16[4,32,256]{2,1,0:T(8,128)(2,1)S(1)}, bf16[4,32,256]{2,1,0:T(8,128)(2,1)S(1)}, bf16[33,4,32,256]{3,2,1,0:T(8,128)(2,1)S(1)}, s32...) while((s32[]{:T(128)}, bf16[4,32,256]{2,1,0:T(8,128)(2,1)S(1)}, ...), condition=%wide.region_1.0_spmd, body=%wide.region_0.0_spmd.sunk | while | flops 10 | bytes 1048865 | solution.py:34
  10.0 3.9 collective-permute-start
  13.9 20.6 %collective-permute-start.1 = (bf16[4,32,256]{2,1,0:T(8,128)(2,1)S(1)}, bf16[4,32,256]{2,1,0:T(8,128)(2,1)S(1)}, u32[]{:S(2)}, u32[]{:S(2)}) collective-permute-start(bf16[4,32,256]{2,1,0:T(8,128)(2,1)S(1)} %get-tuple-element.131), channel_id=1, source_target_pairs={{0,1020},{4,0},{8,4},{12,8},{16,12},{20,16},{24,20},{28,24},{32,28... | collective-permute-start | bytes 196616 | tf_op jit(solution)/shard_map/while/body/eval_jaxpr/ppermute | solution.py:9
  34.5 1.3 collective-permute-done.1
  35.9 1.9 collective-permute-start
  37.8 7.9 collective-permute-start.1
  45.7 1.3 collective-permute-done.1
  47.1 1.9 collective-permute-start
  49.0 7.9 collective-permute-start.1
  58.3 1.9 collective-permute-start
  60.2 7.9 collective-permute-start.1
  68.2 1.3 collective-permute-done.1
  69.5 1.9 collective-permute-start
  71.4 8.0 collective-permute-start.1
  80.8 1.9 collective-permute-start
  82.7 7.9 collective-permute-start.1
  90.7 1.3 collective-permute-done.1
  92.0 1.9 collective-permute-start
  93.9 7.9 collective-permute-start.1
  101.9 1.3 collective-permute-done.1
  103.2 1.9 collective-permute-start
  105.1 7.9 collective-permute-start.1
  113.1 1.3 collective-permute-done.1
  114.4 1.9 collective-permute-start
  116.3 7.9 collective-permute-start.1
  124.3 1.3 collective-permute-done.1
  125.6 1.9 collective-permute-start
  127.5 7.9 collective-permute-start.1
  136.8 1.9 collective-permute-start
  138.7 7.9 collective-permute-start.1
  148.3 1.9 collective-permute-start
  150.3 8.3 collective-permute-start.1
  160.0 1.9 collective-permute-start
  161.9 8.0 collective-permute-start.1
  169.9 1.3 collective-permute-done.1
  171.2 1.9 collective-permute-start
  173.1 7.9 collective-permute-start.1
  182.4 1.9 collective-permute-start
  184.3 7.9 collective-permute-start.1
  192.3 1.3 collective-permute-done.1
  193.6 1.9 collective-permute-start
  195.5 7.9 collective-permute-start.1
  204.8 2.7 gather_fusion
  207.6 4.2 fusion
  211.7 37.3 %all-reduce.5 = bf16[512,256]{1,0:T(8,128)(2,1)S(1)} all-reduce(f32[512,256]{1,0:T(8,128)S(1)} %bitcast.24), channel_id=1, replica_groups=mesh['blk'=256,'rep'=4] {'rep'}, use_global_device_ids=true, to_apply=%region_2.3 | all-reduce | flops 131072 | bytes 786432 | tf_op jit(solution)/shard_map/psum | solution.py:43
  250.9 154.8 %psum.23 = f32[256]{0:T(256)S(1)} all-reduce(f32[256]{0:T(256)S(1)} %get-tuple-element.91), channel_id=1, replica_groups=mesh['blk'=256,'rep'=4] {'blk','rep'}, use_global_device_ids=true, to_apply=%region_5.6 | all-reduce | flops 256 | bytes 2048 | tf_op jit(solution)/shard_map/psum | solution.py:56
  406.2 694.8 %all-reduce.4.cloned.1.call-done = f32[256,256]{1,0:T(8,128)} async-done(((f32[256,256]{1,0:T(8,128)}), f32[256,256]{1,0:T(8,128)}) %all-reduce.4.cloned.1.call-update) | async-done | bytes 262160 | tf_op jit(solution)/shard_map/psum | solution.py:56
  1101.0 1.7 broadcast_multiply_fusion
  (108 shorter events, 14.9 us)
Async XLA Ops:
  7.2 1.0 copy-start
  7.2 1093.9 %all-reduce.4.cloned.1.call-start = ((), (), s32[]{:S(2)}) async-start(), calls=%async_computation | async-start | bytes 524288 | tf_op jit(solution)/shard_map/psum | solution.py:56
  10.0 24.6 %collective-permute-start = (bf16[4,32,256]{2,1,0:T(8,128)(2,1)S(1)}, bf16[4,32,256]{2,1,0:T(8,128)(2,1)S(1)}, u32[]{:S(2)}, u32[]{:S(2)}) collective-permute-start(bf16[4,32,256]{2,1,0:T(8,128)(2,1)S(1)} %get-tuple-element.130), channel_id=1, source_target_pairs={{0,4},{4,8},{8,12},{12,16},{16,20},{20,24},{24,28},{28,32},{32,36}... | collective-permute-start | bytes 196616 | tf_op jit(solution)/shard_map/while/body/eval_jaxpr/ppermute | solution.py:9
  13.9 21.9 %collective-permute-start.1 = (bf16[4,32,256]{2,1,0:T(8,128)(2,1)S(1)}, bf16[4,32,256]{2,1,0:T(8,128)(2,1)S(1)}, u32[]{:S(2)}, u32[]{:S(2)}) collective-permute-start(bf16[4,32,256]{2,1,0:T(8,128)(2,1)S(1)} %get-tuple-element.131), channel_id=1, source_target_pairs={{0,1020},{4,0},{8,4},{12,8},{16,12},{20,16},{24,20},{28,24},{32,28... | collective-permute-start | bytes 196616 | tf_op jit(solution)/shard_map/while/body/eval_jaxpr/ppermute | solution.py:9
  35.9 9.9 collective-permute-start
  37.8 9.2 collective-permute-start.1
  47.1 9.9 collective-permute-start
  49.0 9.2 collective-permute-start.1
  58.3 9.9 collective-permute-start
  60.2 9.2 collective-permute-start.1
  69.5 10.0 collective-permute-start
  71.4 9.3 collective-permute-start.1
  80.8 9.9 collective-permute-start
  82.7 9.2 collective-permute-start.1
  92.0 9.9 collective-permute-start
  93.9 9.2 collective-permute-start.1
  103.2 9.9 collective-permute-start
  105.1 9.2 collective-permute-start.1
  114.4 9.9 collective-permute-start
  116.3 9.2 collective-permute-start.1
  125.6 9.9 collective-permute-start
  127.5 9.2 collective-permute-start.1
  136.8 10.5 collective-permute-start
  138.7 9.5 collective-permute-start.1
  148.3 10.3 collective-permute-start
  150.3 9.6 collective-permute-start.1
  160.0 9.9 collective-permute-start
  161.9 9.3 collective-permute-start.1
  171.2 9.9 collective-permute-start
  173.1 9.2 collective-permute-start.1
  182.4 9.9 collective-permute-start
  184.3 9.2 collective-permute-start.1
  193.6 9.9 collective-permute-start
  195.5 9.2 collective-permute-start.1
  207.6 41.5 %copy-start.1 = (bf16[256,256]{1,0:T(8,128)(2,1)S(1)}, bf16[256,256]{1,0:T(8,128)(2,1)}, u32[]{:S(2)}) copy-start(bf16[256,256]{1,0:T(8,128)(2,1)} %param.13) | copy-start | bytes 393220
  207.6 41.5 %copy-start.2 = (bf16[128,256]{1,0:T(8,128)(2,1)S(1)}, bf16[128,256]{1,0:T(8,128)(2,1)}, u32[]{:S(2)}) copy-start(bf16[128,256]{1,0:T(8,128)(2,1)} %param.15) | copy-start | bytes 196612
  207.6 41.5 %copy-start.3 = (f32[256]{0:T(256)S(1)}, f32[256]{0:T(256)}, u32[]{:S(2)}) copy-start(f32[256]{0:T(256)} %param.14) | copy-start | bytes 3076
Sparse Core Ops, SparseCore 0:
  251.0 849.9 all-reduce.3
where the time goes:
time: 1110 us
  waiting for transfers between devices  716 us (65%)
  blocking collectives  192 us (17%)
  starting transfers between devices  173 us (16%)
  between operations  14.1 us (1%)
    psum x1, waiting for transfers between devices, body(): lax.psum((local_weight, local_bias), ('blk', 'rep'))  695 us
    ppermute x32, starting transfers between devices, from_behind(): lax.ppermute(x, axis, [(i, (i + by) % length) for i in range(length)])  173 us
    psum x1, blocking collectives, body(): lax.psum((local_weight, local_bias), ('blk', 'rep'))  155 us
    psum x1, blocking collectives, body(): totals = lax.psum(partial_sum, 'rep')  37.3 us
  transfers between devices with their start and end apart: 33, of which 18 were waited for; matrix products, arithmetic and copies ran while one was open for 0% of the time, Pallas kernels for 0%

commit v1 on v0

v1 whole, which is shorter than its diff:
```python
import math

import jax
import jax.numpy as jnp
from jax import lax
from jax.experimental import pallas as pl
from jax.experimental.pallas import tpu as pltpu
from jax.sharding import PartitionSpec as P

STEPS = 8
ZL = 8
ZH = 4
Y = 4
X = 4
STOP = 99


def dev(b, r):
    return {"blk": b, "rep": r}


def rcopy(src, dst, ssem, rsem, to):
    return pltpu.make_async_remote_copy(
        src_ref=src,
        dst_ref=dst,
        send_sem=ssem,
        recv_sem=rsem,
        device_id=to,
        device_id_type=pl.DeviceIdType.MESH,
    )


def kernel(
    cols,
    cnt,
    feat,
    vals,
    weight,
    bias,
    cot,
    act_out,
    wg_out,
    bg_out,
    win,
    vv,
    wv,
    bv,
    cv,
    actv,
    send1,
    got1,
    mine,
    got2,
    buf_a,
    got_a,
    buf_b,
    got_b,
    buf_c,
    got_c,
    buf_d,
    got_d,
    got_e,
    rows_f,
    full,
    bias_v,
    load_sem,
    hs,
    hr,
    xs,
    xr,
    ps,
    pr,
    rs,
    rr,
    as_,
    ar,
):
    b = lax.axis_index("blk")
    r = lax.axis_index("rep")
    n_blk = 256
    xl = b % 2
    z = (b // 2) % 32
    y = b // 64
    xh = r // 2
    core = r % 2
    x = xh * 2 + xl
    zl = z % ZL
    zh = z // ZL
    up = lax.rem(b + 2, n_blk)
    down = lax.rem(b + n_blk - 2, n_blk)
    across = b + 1 - 2 * xl
    sibling = r + 1 - 2 * core
    far = lax.rem(r + 2, 4)

    def x_dev(q):
        return dev(b - xl + q % 2, (q // 2) * 2 + core)

    def y_dev(w):
        return dev(w * 64 + b % 64, r)

    def zl_dev(j):
        return dev(y * 64 + (zh * ZL + j) * 2 + xl, r)

    def zh_dev(j):
        return dev(y * 64 + (j * ZL + zl) * 2 + xl, r)

    barrier = pltpu.get_barrier_semaphore()
    partners = [dev(up, r), dev(down, r), dev(b, sibling)]
    partners += [x_dev(lax.rem(x + u, X)) for u in range(1, X)]
    partners += [y_dev(lax.rem(y + u, Y)) for u in range(1, Y)]
    partners += [zl_dev(lax.rem(zl + u, ZL)) for u in range(1, ZL)]
    partners += [zh_dev(lax.rem(zh + u, ZH)) for u in range(1, ZH)]
    load_own = pltpu.make_async_copy(
        feat.at[:, pl.ds(pl.multiple_of(r * 32, 32), 32), :], win.at[pl.ds(8 * 8 + 4, 4)], load_sem.at[0]
    )
    load_own.start()
    for to in partners:
        pl.semaphore_signal(barrier, inc=1, device_id=to, device_id_type=pl.DeviceIdType.MESH)
    loads = [
        pltpu.make_async_copy(vals, vv, load_sem.at[1]),
        pltpu.make_async_copy(weight, wv, load_sem.at[2]),
        pltpu.make_async_copy(bias, bv, load_sem.at[3]),
        pltpu.make_async_copy(cot, cv, load_sem.at[4]),
    ]
    for c in loads:
        c.start()
    load_own.wait()
    pl.semaphore_wait(barrier, len(partners))

    def chain(direction, k, chunk):
        off = -k if direction == 0 else k
        to = off - 1 if direction == 0 else off + 1
        first, count = (5, 3) if chunk == 0 else (3, 2)
        return rcopy(
            win.at[pl.ds((off + 8) * 8 + first, count)],
            win.at[pl.ds((to + 8) * 8 + first, count)],
            hs.at[direction, chunk, k],
            hr.at[direction, chunk, k],
            dev(up if direction == 0 else down, r),
        )

    def relay(off, sem):
        return rcopy(
            win.at[pl.ds((off + 8) * 8 + 5, 3)],
            win.at[pl.ds((off + 8) * 8, 3)],
            xs.at[sem],
            xr.at[sem],
            dev(across, r),
        )

    swap = rcopy(win.at[pl.ds(68, 1)], win.at[pl.ds(67, 1)], xs.at[17], xr.at[17], dev(across, r))
    swap.start()
    chain(0, 0, 0).start()
    chain(1, 0, 0).start()
    relay(0, 8).start()
    swap.wait_recv()
    chain(0, 0, 1).start()
    chain(1, 0, 1).start()

    def step(k, _):
        for direction in (0, 1):
            off = -k if direction == 0 else k
            chain(direction, k - 1, 0).wait_recv()
            chain(direction, k, 0).start()
            relay(off, 8 + off).start()
        for direction in (0, 1):
            chain(direction, k - 1, 1).wait_recv()
            chain(direction, k, 1).start()
        return 0

    lax.fori_loop(1, STEPS, step, 0)
    for direction in (0, 1):
        chain(direction, STEPS - 1, 0).wait_recv()
    last = relay(8 - 16 * xl, 0)
    last.start()
    for direction in (0, 1):
        chain(direction, STEPS - 1, 1).wait_recv()
    for c in loads:
        c.wait()

    def relayed(k, _):
        relay(k - 8, k).wait_recv()
        return 0

    lax.fori_loop(1, 16, relayed, 0)
    last.wait_recv()

    def sent(k, _):
        for direction in (0, 1):
            for chunk in (0, 1):
                chain(direction, k, chunk).wait_send()
        return 0

    lax.fori_loop(0, STEPS, sent, 0)

    def relay_sent(k, _):
        relay(k - 8, k).wait_send()
        return 0

    lax.fori_loop(1, 16, relay_sent, 0)
    last.wait_send()
    swap.wait_send()

    slots = 64
    lane_slot = lax.broadcasted_iota(jnp.int32, (8, 32, 128), 0)

    def place(j, s):
        col = cols[j, s]
        e = (col // 4 - b + 16 + n_blk) % n_blk
        t = col % 4
        kk = (e + xl) // 2
        tile = jnp.where(e % 2 == 1, (t + 3) % 4, 4 + t)
        return jnp.minimum(kk * 8 + tile, 135)

    def partial(j):
        count = cnt[j]

        def chunk(c, acc):
            first = c * 8
            picked = jnp.concatenate([win[place(j, first + u)] for u in range(8)], axis=0)
            v = vv[j, pl.ds(first, 8)]
            v = jnp.where(lane_slot + first < count, v, jnp.zeros_like(v)).reshape(256, 128)
            return acc + lax.dot_general(
                v, picked, (((0,), (0,)), ((), ())), preferred_element_type=jnp.float32
            )

        return lax.fori_loop(0, slots // 8, chunk, jnp.zeros((128, 256), jnp.float32))

    to_sibling = []
    for h in (0, 1):
        if STOP > 1:
            send1[h] = partial(h * 2 + 1 - core)
        c = rcopy(send1.at[h], got1.at[h], ps.at[h], pr.at[h], dev(b, sibling))
        c.start()
        to_sibling.append(c)
    for h in (0, 1):
        if STOP > 1:
            mine[h] = partial(h * 2 + core)
    for h in (0, 1):
        to_sibling[h].wait_recv()
    mine[...] = mine[...] + got1[...]
    c = rcopy(mine.at[1 - xh], got2, ps.at[2], pr.at[2], dev(b, far))
    c.start()
    c.wait()
    for h in (0, 1):
        to_sibling[h].wait_send()

    agg = (mine[xh] + got2[...]).astype(jnp.bfloat16)
    pre = jnp.dot(agg, wv[...], preferred_element_type=jnp.float32) + bv[...]
    sig = 1.0 / (1.0 + jnp.exp(-pre))
    actv[...] = (pre * sig).astype(jnp.bfloat16)
    store_act = pltpu.make_async_copy(actv, act_out, load_sem.at[0])
    store_act.start()
    grad = (cv[...].astype(jnp.float32) * sig * (1.0 + pre * (1.0 - sig))).astype(jnp.bfloat16)
    bias_row = jnp.sum(grad.astype(jnp.float32), axis=0, keepdims=True)
    for h in (0, 1):
        buf_a[h, :128] = lax.dot_general(
            agg[:, h * 128 : (h + 1) * 128],
            grad,
            (((0,), (0,)), ((), ())),
            preferred_element_type=jnp.float32,
        )
        buf_a[h, 128:] = jnp.broadcast_to(bias_row, (8, 256))

    pending = []

    def swap_all(n, me, dev_of, src, dst, base):
        copies = []
        for u in range(1, n):
            p = lax.rem(me + u, n)
            c = rcopy(src(p), dst, as_.at[base + u], ar.at[base + u], dev_of(p))
            c.start()
            copies.append(c)
        for c in copies:
            c.wait_recv()
        pending.extend(copies)

    c = rcopy(buf_a.at[1 - core], got_a, as_.at[0], ar.at[0], dev(b, sibling))
    c.start()
    c.wait_recv()
    pending.append(c)
    total = buf_a[core] + got_a[...]
    for q in range(X):
        buf_b[q, :32] = total[q * 32 : (q + 1) * 32]
        buf_b[q, 32:] = total[128:]
    got_b[x] = buf_b[x]
    swap_all(X, x, x_dev, lambda p: buf_b.at[p], got_b.at[x], 0)
    total = got_b[0] + got_b[1] + got_b[2] + got_b[3]
    for w in range(Y):
        buf_c[w, :8] = total[w * 8 : (w + 1) * 8]
        buf_c[w, 8:] = total[32:]
    got_c[y] = buf_c[y]
    swap_all(Y, y, y_dev, lambda p: buf_c.at[p], got_c.at[y], 4)
    total = got_c[0] + got_c[1] + got_c[2] + got_c[3]
    for j in range(ZL):
        buf_d[j, 0:1] = total[j : j + 1]
        buf_d[j, 1:2] = total[8:9]
    got_d[zl] = buf_d[zl]
    swap_all(ZL, zl, zl_dev, lambda p: buf_d.at[p], got_d.at[zl], 8)
    total = got_d[0]
    for j in range(1, ZL):
        total = total + got_d[j]
    got_e[zh] = total
    swap_all(ZH, zh, zh_dev, lambda p: got_e.at[zh], got_e.at[zh], 16)
    total = (got_e[0] + got_e[1] + got_e[2] + got_e[3]) * (1.0 / math.sqrt(131072.0))
    bias_v[...] = total[1:2]
    store_bias = pltpu.make_async_copy(bias_v, bg_out, load_sem.at[1])
    store_bias.start()
    rows_f[zl] = total[0:1]
    swap_all(ZL, zl, zl_dev, lambda p: rows_f.at[zl], rows_f.at[zl], 20)
    at = core * 16 + x * 4 + y
    full[at] = jnp.concatenate([rows_f[j] for j in range(ZL)], axis=0)
    swap_all(Y, y, y_dev, lambda p: full.at[at], full.at[at], 28)
    mid = full.at[pl.ds(core * 16 + x * 4, 4)]
    swap_all(X, x, x_dev, lambda p: mid, mid, 32)
    half = full.at[pl.ds(core * 16, 16)]
    c = rcopy(half, half, as_.at[32], ar.at[32], dev(b, sibling))
    c.start()
    c.wait()
    store_full = pltpu.make_async_copy(full, wg_out, load_sem.at[2])
    store_full.start()
    for c in pending:
        c.wait_send()
    store_act.wait()
    store_bias.wait()
    store_full.wait()


def body(features, tile_vals, tile_cols, tile_count, weight, bias, cotangent):
    f32, bf16 = jnp.float32, jnp.bfloat16
    any_ = pl.BlockSpec(memory_space=pl.ANY)
    smem = pl.BlockSpec(memory_space=pltpu.SMEM)
    act, wg, bg = pl.pallas_call(
        kernel,
        out_shape=[
            jax.ShapeDtypeStruct((128, 256), bf16),
            jax.ShapeDtypeStruct((32, 8, 256), f32),
            jax.ShapeDtypeStruct((1, 256), f32),
        ],
        in_specs=[smem, smem, any_, any_, any_, any_, any_],
        out_specs=[any_, any_, any_],
        scratch_shapes=[
            pltpu.VMEM((17 * 8, 32, 256), bf16),
            pltpu.VMEM((4, 64, 32, 128), bf16),
            pltpu.VMEM((256, 256), bf16),
            pltpu.VMEM((1, 256), f32),
            pltpu.VMEM((128, 256), bf16),
            pltpu.VMEM((128, 256), bf16),
            pltpu.VMEM((2, 128, 256), f32),
            pltpu.VMEM((2, 128, 256), f32),
            pltpu.VMEM((2, 128, 256), f32),
            pltpu.VMEM((128, 256), f32),
            pltpu.VMEM((2, 136, 256), f32),
            pltpu.VMEM((136, 256), f32),
            pltpu.VMEM((4, 40, 256), f32),
            pltpu.VMEM((4, 40, 256), f32),
            pltpu.VMEM((4, 16, 256), f32),
            pltpu.VMEM((4, 16, 256), f32),
            pltpu.VMEM((8, 2, 256), f32),
            pltpu.VMEM((8, 2, 256), f32),
            pltpu.VMEM((4, 2, 256), f32),
            pltpu.VMEM((8, 1, 256), f32),
            pltpu.VMEM((32, 8, 256), f32),
            pltpu.VMEM((1, 256), f32),
            pltpu.SemaphoreType.DMA((5,)),
            pltpu.SemaphoreType.DMA((2, 2, STEPS)),
            pltpu.SemaphoreType.DMA((2, 2, STEPS)),
            pltpu.SemaphoreType.DMA((18,)),
            pltpu.SemaphoreType.DMA((18,)),
            pltpu.SemaphoreType.DMA((3,)),
            pltpu.SemaphoreType.DMA((3,)),
            pltpu.SemaphoreType.DMA((1,)),
            pltpu.SemaphoreType.DMA((1,)),
            pltpu.SemaphoreType.DMA((36,)),
            pltpu.SemaphoreType.DMA((36,)),
        ],
        compiler_params=pltpu.CompilerParams(
            collective_id=0, has_side_effects=True, vmem_limit_bytes=32 * 1024 * 1024
        ),
    )(
        tile_cols,
        tile_count,
        features.reshape(4, 128, 256),
        tile_vals,
        weight,
        bias.reshape(1, 256),
        cotangent,
    )
    return act, wg.reshape(256, 256), bg.reshape(256)


def solution(mesh):
    return jax.shard_map(
        body,
        mesh=mesh,
        in_specs=(
            P("blk", None),
            P("blk", None, "rep", None),
            P("blk", None),
            P("blk"),
            P(),
            P(),
            P(("blk", "rep"), None),
        ),
        out_specs=(P(("blk", "rep"), None), P(), P()),
        check_vma=False,
    )
```

time: 1110 us -> 128 us (0.12)
  waiting for transfers between devices: 716 us -> 0 us
  blocking collectives: 192 us -> 0 us
  starting transfers between devices: 173 us -> 0 us
  Pallas kernels: 0 us -> 119 us
  between operations: 14.1 us -> 0.66 us
    psum x1 -> x0, waiting for transfers between devices: 695 us -> none  [body(): lax.psum((local_weight, local_bias), ('blk', 'rep'))]
    psum x2 -> x0, blocking collectives: 192 us -> none  [the longest x1 155 us: body(): lax.psum((local_weight, local_bias), ('blk', 'rep'))]
    ppermute x32 -> x0, starting transfers between devices: 173 us -> none  [from_behind(): lax.ppermute(x, axis, [(i, (i + by) % length) for i in range(length)])]
    pallas_call x0 -> x1, Pallas kernels: none -> 119 us  [body(): pl.pallas_call(kernel, out_shape=[jax.ShapeDtypeStruct((128, 256), bf16),...]
    ppermute x32 -> x0, waiting for transfers between devices: 20.7 us -> none  [from_behind(): lax.ppermute(x, axis, [(i, (i + by) % length) for i in range(length)])]
  transfers between devices with their start and end apart: 33 -> 0, of which waited for: 18 -> 0; matrix products, arithmetic and copies ran while one was open for 0% -> 0% of each run, Pallas kernels for 0% -> 0%
where the time goes in v1:
time: 128 us
  Pallas kernels  119 us (93%)
  local copies, waits for them, and re-layouts  8.19 us (6%)
    pallas_call x1, Pallas kernels, body(): pl.pallas_call(kernel, out_shape=[jax.ShapeDtypeStruct((128, 256), bf16),...  119 us
    unnamed x17, local copies, waits for them, and re-layouts  8.19 us

profile of v1, /device:TPU:1, one launch (start us, length us, event | category | flops | bytes accessed | tf_op | source)
XLA Modules:
  0.0 127.9 jit_solution(94030888700891741)
XLA Ops:
  0.6 0.0 copy-start
  0.6 1.6 %copy-done = bf16[4,64,32,128]{3,2,1,0:T(8,128)(2,1)S(1)} copy-done((bf16[4,64,32,128]{3,2,1,0:T(8,128)(2,1)S(1)}, bf16[4,64,32,128]{3,2,1,0:T(8,128)(2,1)}, u32[]{:S(2)}) %copy-start) | copy-done | bytes 2097176
  2.2 0.0 copy-start.1
  2.2 0.9 copy-done.1
  3.2 0.0 copy-start.2
  3.2 0.9 copy-done.2
  4.1 0.0 copy-start.3
  4.1 0.8 copy-done.3
  4.9 0.0 copy-start.4
  4.9 0.7 copy-done.4
  5.6 0.0 copy-start.5
  5.6 0.7 copy-done.5
  6.3 0.0 copy-start.6
  6.3 0.7 copy-done.6
  6.9 119.1 %shard_map.94 = (bf16[128,256]{1,0:T(8,128)(2,1)S(1)}, f32[32,8,256]{2,1,0:T(8,128)S(1)}, f32[1,256]{1,0:T(1,128)S(1)}) custom-call(s32[4,64]{1,0:T(4,128)S(1)} %copy-done.4, s32[4]{0:T(128)S(1)} %copy-done.6, bf16[4,128,256]{2,1,0:T(8,128)(2,1)S(1)} %bitcast.4, bf16[4,64,32,128]{3,2,1,0:T(8,128)(2,1)S(1)} %copy-done, bf16[256,256]{1,0:T(8,128)(2,1)S(1)} %copy-done.2, ...), custom_call_target="tpu_custom_call" | custom-call | tf_op jit(solution)/shard_map/pallas_call | solution.py:333
  126.0 0.6 copy.13
  126.6 0.7 copy.14
  127.3 0.6 copy.15
Async XLA Ops:
  0.6 1.6 %copy-start = (bf16[4,64,32,128]{3,2,1,0:T(8,128)(2,1)S(1)}, bf16[4,64,32,128]{3,2,1,0:T(8,128)(2,1)}, u32[]{:S(2)}) copy-start(bf16[4,64,32,128]{3,2,1,0:T(8,128)(2,1)} %vals.1) | copy-start | bytes 6291460
  2.2 0.9 copy-start.1
  3.2 0.9 copy-start.2
  4.1 0.8 copy-start.3
  4.9 0.7 copy-start.4
  5.6 0.7 copy-start.5
  6.3 0.7 copy-start.6

commit v2 on v1

v2 whole, which is shorter than its diff:
```python
import math

import jax
import jax.numpy as jnp
from jax import lax
from jax.experimental import pallas as pl
from jax.experimental.pallas import tpu as pltpu
from jax.sharding import PartitionSpec as P

STEPS = 8
ZL = 4
ZH = 8
XY = 16
Q = 64
RELAYED = ((Q, 96), (Q + 96, 96))
PLAIN = ((-Q, 2 * Q),)
STOP = 99


def dev(b, r):
    return {"blk": b, "rep": r}


def rcopy(src, dst, ssem, rsem, to):
    return pltpu.make_async_remote_copy(
        src_ref=src,
        dst_ref=dst,
        send_sem=ssem,
        recv_sem=rsem,
        device_id=to,
        device_id_type=pl.DeviceIdType.MESH,
    )


def kernel(
    cols,
    cnt,
    feat,
    vals,
    weight,
    bias,
    cot,
    act_out,
    wg_out,
    bg_out,
    own,
    win,
    vv,
    where_v,
    where_s,
    acc,
    wv,
    bv,
    cv,
    actv,
    got1,
    mine,
    got2,
    buf_a,
    got_a,
    buf_b,
    got_b,
    buf_d,
    got_d,
    got_e,
    rows_f,
    full,
    bias_v,
    load_sem,
    hs,
    hr,
    xs,
    xr,
    ps,
    pr,
    as_,
    ar,
):
    b = lax.axis_index("blk")
    r = lax.axis_index("rep")
    n_blk = 256
    xl = b % 2
    z = (b // 2) % 32
    y = b // 64
    xh = r // 2
    core = r % 2
    x = xh * 2 + xl
    xy = x * 4 + y
    zl = z % ZL
    zh = z // ZL
    up = lax.rem(b + 2, n_blk)
    down = lax.rem(b + n_blk - 2, n_blk)
    across = b + 1 - 2 * xl
    sibling = r + 1 - 2 * core
    far = lax.rem(r + 2, 4)

    def xy_dev(q):
        return dev((q % 4) * 64 + z * 2 + (q // 4) % 2, (q // 8) * 2 + core)

    def zl_dev(j):
        return dev(y * 64 + (zh * ZL + j) * 2 + xl, r)

    def zh_dev(j):
        return dev(y * 64 + (j * ZL + zl) * 2 + xl, r)

    load_own = pltpu.make_async_copy(
        feat.at[:, pl.ds(pl.multiple_of(r * 32, 32), 32), :], own, load_sem.at[0]
    )
    load_own.start()
    barrier = pltpu.get_barrier_semaphore()
    partners = [dev(up, r), dev(down, r), dev(b, sibling)]
    partners += [zl_dev(lax.rem(zl + u, ZL)) for u in range(1, ZL)]
    partners += [zh_dev(lax.rem(zh + u, ZH)) for u in range(1, ZH)]
    partners += [xy_dev(lax.rem(xy + u, XY)) for u in range(1, XY)]
    for to in partners:
        pl.semaphore_signal(barrier, inc=1, device_id=to, device_id_type=pl.DeviceIdType.MESH)
    loads = [
        pltpu.make_async_copy(vals, vv.at[:, pl.ds(0, 64)], load_sem.at[1]),
        pltpu.make_async_copy(weight, wv, load_sem.at[2]),
        pltpu.make_async_copy(bias, bv, load_sem.at[3]),
        pltpu.make_async_copy(cot, cv, load_sem.at[4]),
    ]
    for c in loads:
        c.start()

    load_own.wait()
    win[8, 256:] = own[...].reshape(128, 256).T
    win[16 * (1 - xl), : 256 - Q] = jnp.zeros((256 - Q, 128), jnp.bfloat16)
    for j in range(4):
        vv[j, 64] = jnp.zeros((32, 128), jnp.bfloat16)
    acc[...] = jnp.zeros_like(acc)

    lane = lax.broadcasted_iota(jnp.int32, (1, 256), 1)

    def note_slot(s, found):
        out = []
        for j in range(4):
            col = cols[j, s]
            e = ((col >> 2) - b + 16 + n_blk) & (n_blk - 1)
            at = ((e + xl) >> 1) * 8 + (e & 1) * 4 + (col & 3)
            at = jnp.where(s < cnt[j], at, 1000)
            out.append(jnp.where(lane == at, s, found[j]))
        return tuple(out)

    found = lax.fori_loop(0, 64, note_slot, (jnp.full((1, 256), 64, jnp.int32),) * 4)
    for j in range(4):
        where_v[j : j + 1] = found[j]
    note = pltpu.make_async_copy(where_v, where_s, load_sem.at[5])
    note.start()
    pl.semaphore_wait(barrier, len(partners))

    def chain(direction, k, n):
        off = -k if direction == 0 else k
        to = off - 1 if direction == 0 else off + 1
        first, count = (RELAYED + PLAIN)[n]
        return rcopy(
            win.at[off + 8, pl.ds(256 + first, count)],
            win.at[to + 8, pl.ds(256 + first, count)],
            hs.at[direction, n, k],
            hr.at[direction, n, k],
            dev(up if direction == 0 else down, r),
        )

    def relay(off, n, sem):
        first, count = RELAYED[n]
        return rcopy(
            win.at[off + 8, pl.ds(256 + first, count)],
            win.at[off + 8, pl.ds(first - Q, count)],
            xs.at[n, sem],
            xr.at[n, sem],
            dev(across, r),
        )

    n_rel = len(RELAYED)
    n_all = n_rel + len(PLAIN)
    swap = rcopy(
        win.at[8, pl.ds(256, Q)], win.at[8, pl.ds(256 - Q, Q)], xs.at[0, 17], xr.at[0, 17], dev(across, r)
    )
    swap.start()
    for n in range(n_rel):
        chain(0, 0, n).start()
        chain(1, 0, n).start()
        relay(0, n, 8).start()
    swap.wait_recv()
    for n in range(n_rel, n_all):
        chain(0, 0, n).start()
        chain(1, 0, n).start()
    for c in loads:
        c.wait()
    note.wait()

    def products(places):
        left = []
        for at in places:
            left.append(win[at, 256:])
            left.append(jnp.concatenate([win[at, 256 - Q : 256], win[at, : 256 - Q]], axis=0))
        left = jnp.concatenate(left, axis=1)
        for pair in (0, 1):
            right = []
            for j in (2 * pair, 2 * pair + 1):
                tiles = [vv[j, where_s[j, at * 8 + u]] for at in places for u in range(8)]
                right.append(jnp.concatenate(tiles, axis=0))
            right = jnp.concatenate(right, axis=1)
            out = jnp.dot(left, right, preferred_element_type=jnp.float32)
            acc[2 * pair] += out[:, :128]
            acc[2 * pair + 1] += out[:, 128:]
            if len(places) > 1:
                yield pair

    def relays_in(k):
        for n in range(n_rel):
            relay(-k, n, 8 - k).wait_recv()
            relay(k, n, 8 + k).wait_recv()

    def step(k, _):
        for n in range(n_rel):
            for direction in (0, 1):
                off = -k if direction == 0 else k
                chain(direction, k - 1, n).wait_recv()
                chain(direction, k, n).start()
                relay(off, n, 8 + off).start()
        for n in range(n_rel, n_all):
            for direction in (0, 1):
                chain(direction, k - 1, n).wait_recv()
                chain(direction, k, n).start()

        @pl.when(k > 1)
        def _():
            relays_in(k - 1)
            for _ in products([8 - (k - 1)]):
                pass
            for _ in products([8 + (k - 1)]):
                pass

        return 0

    for n in range(n_rel):
        relay(0, n, 8).wait_recv()
    for _ in products([8]):
        pass
    lax.fori_loop(1, STEPS, step, 0)
    lasts = []
    for n in range(n_rel):
        for direction in (0, 1):
            chain(direction, STEPS - 1, n).wait_recv()
        lasts.append(relay(8 - 16 * xl, n, 0))
        lasts[-1].start()
    relays_in(STEPS - 1)
    for _ in products([1]):
        pass
    for _ in products([15]):
        pass
    for n in range(n_rel, n_all):
        for direction in (0, 1):
            chain(direction, STEPS - 1, n).wait_recv()
    for c in lasts:
        c.wait_recv()
    to_sibling = []
    for pair in products([0, 16]):
        c = rcopy(acc.at[2 * pair + 1 - core], got1.at[pair], ps.at[pair], pr.at[pair], dev(b, sibling))
        c.start()
        to_sibling.append(c)
    other = 1 - xh
    to_sibling[0].wait_recv()
    to_sibling[1].wait_recv()
    mine[...] = acc[2 * other + core] + got1[other]
    c = rcopy(mine, got2, ps.at[2], pr.at[2], dev(b, far))
    c.start()
    kept = acc[2 * xh + core] + got1[xh]

    def sent(k, _):
        for direction in (0, 1):
            for n in range(n_all):
                chain(direction, k, n).wait_send()
        return 0

    lax.fori_loop(0, STEPS, sent, 0)

    def relay_sent(k, _):
        for n in range(n_rel):
            relay(k - 8, n, k).wait_send()
        return 0

    lax.fori_loop(1, 16, relay_sent, 0)
    for d in lasts:
        d.wait_send()
    swap.wait_send()
    for d in to_sibling:
        d.wait_send()
    c.wait()

    agg = (kept + got2[...]).astype(jnp.bfloat16)
    pre = (
        lax.dot_general(
            agg, wv[...], (((0,), (0,)), ((), ())), preferred_element_type=jnp.float32
        )
        + bv[...]
    )
    sig = 1.0 / (1.0 + jnp.exp(-pre))
    grad = (cv[...].astype(jnp.float32) * sig * (1.0 + pre * (1.0 - sig))).astype(jnp.bfloat16)
    bias_row = jnp.sum(grad.astype(jnp.float32), axis=0, keepdims=True)
    for h in (0, 1):
        buf_a[h, :128] = jnp.dot(
            agg[h * 128 : (h + 1) * 128], grad, preferred_element_type=jnp.float32
        )
        buf_a[h, 128:] = jnp.broadcast_to(bias_row, (8, 256))

    pending = []

    def swap_all(n, me, dev_of, src, dst, base):
        copies = []
        for u in range(1, n):
            p = lax.rem(me + u, n)
            c = rcopy(src(p), dst, as_.at[base + u], ar.at[base + u], dev_of(p))
            c.start()
            copies.append(c)
        for c in copies:
            c.wait_recv()
        pending.extend(copies)

    c = rcopy(buf_a.at[1 - core], got_a, as_.at[0], ar.at[0], dev(b, sibling))
    c.start()
    pending.append(c)
    actv[...] = (pre * sig).astype(jnp.bfloat16)
    store_act = pltpu.make_async_copy(actv, act_out, load_sem.at[0])
    store_act.start()
    c.wait_recv()
    total = buf_a[core] + got_a[...]
    for q in range(XY):
        buf_b[q, :8] = total[q * 8 : (q + 1) * 8]
        buf_b[q, 8:] = total[128:]
    got_b[xy] = buf_b[xy]
    swap_all(XY, xy, xy_dev, lambda p: buf_b.at[p], got_b.at[xy], 0)
    total = got_b[0]
    for q in range(1, XY):
        total = total + got_b[q]
    for j in range(ZL):
        buf_d[j, 0:2] = total[2 * j : 2 * j + 2]
        buf_d[j, 2:3] = total[8:9]
    got_d[zl] = buf_d[zl]
    swap_all(ZL, zl, zl_dev, lambda p: buf_d.at[p], got_d.at[zl], 16)
    total = got_d[0]
    for j in range(1, ZL):
        total = total + got_d[j]
    got_e[zh] = total
    swap_all(ZH, zh, zh_dev, lambda p: got_e.at[zh], got_e.at[zh], 20)
    total = got_e[0]
    for j in range(1, ZH):
        total = total + got_e[j]
    total = total * (1.0 / math.sqrt(131072.0))
    rows_f[zl] = total[0:2]
    bias_v[...] = total[2:3]
    store_bias = pltpu.make_async_copy(bias_v, bg_out, load_sem.at[1])
    store_bias.start()
    swap_all(ZL, zl, zl_dev, lambda p: rows_f.at[zl], rows_f.at[zl], 28)
    at = core * XY + xy
    full[at] = jnp.concatenate([rows_f[j] for j in range(ZL)], axis=0)
    swap_all(XY, xy, xy_dev, lambda p: full.at[at], full.at[at], 32)
    half = full.at[pl.ds(core * XY, XY)]
    c = rcopy(half, half, as_.at[32], ar.at[32], dev(b, sibling))
    c.start()
    c.wait()
    store_full = pltpu.make_async_copy(full, wg_out, load_sem.at[2])
    store_full.start()
    for c in pending:
        c.wait_send()
    store_act.wait()
    store_bias.wait()
    store_full.wait()


def hand_over(a, b, c, a_out, b_out, c_out, sem):
    copies = [
        pltpu.make_async_copy(a, a_out, sem.at[0]),
        pltpu.make_async_copy(b, b_out, sem.at[1]),
        pltpu.make_async_copy(c, c_out, sem.at[2]),
    ]
    for d in copies:
        d.start()
    for d in copies:
        d.wait()


def body(features, tile_vals, tile_cols, tile_count, weight, bias, cotangent):
    f32, bf16 = jnp.float32, jnp.bfloat16
    any_ = pl.BlockSpec(memory_space=pl.ANY)
    smem = pl.BlockSpec(memory_space=pltpu.SMEM)
    act, wg, bg = pl.pallas_call(
        kernel,
        out_shape=[
            jax.ShapeDtypeStruct((128, 256), bf16),
            jax.ShapeDtypeStruct((32, 8, 256), f32),
            jax.ShapeDtypeStruct((1, 256), f32),
        ],
        in_specs=[smem, smem, any_, any_, any_, any_, any_],
        out_specs=[any_, any_, any_],
        scratch_shapes=[
            pltpu.VMEM((4, 32, 256), bf16),
            pltpu.VMEM((17, 512, 128), bf16),
            pltpu.VMEM((4, 65, 32, 128), bf16),
            pltpu.VMEM((4, 256), jnp.int32),
            pltpu.SMEM((4, 256), jnp.int32),
            pltpu.VMEM((4, 256, 128), f32),
            pltpu.VMEM((256, 256), bf16),
            pltpu.VMEM((1, 256), f32),
            pltpu.VMEM((128, 256), bf16),
            pltpu.VMEM((128, 256), bf16),
            pltpu.VMEM((2, 256, 128), f32),
            pltpu.VMEM((256, 128), f32),
            pltpu.VMEM((256, 128), f32),
            pltpu.VMEM((2, 136, 256), f32),
            pltpu.VMEM((136, 256), f32),
            pltpu.VMEM((XY, 16, 256), f32),
            pltpu.VMEM((XY, 16, 256), f32),
            pltpu.VMEM((ZL, 3, 256), f32),
            pltpu.VMEM((ZL, 3, 256), f32),
            pltpu.VMEM((ZH, 3, 256), f32),
            pltpu.VMEM((ZL, 2, 256), f32),
            pltpu.VMEM((32, 8, 256), f32),
            pltpu.VMEM((1, 256), f32),
            pltpu.SemaphoreType.DMA((6,)),
            pltpu.SemaphoreType.DMA((2, len(RELAYED + PLAIN), STEPS)),
            pltpu.SemaphoreType.DMA((2, len(RELAYED + PLAIN), STEPS)),
            pltpu.SemaphoreType.DMA((len(RELAYED), 18)),
            pltpu.SemaphoreType.DMA((len(RELAYED), 18)),
            pltpu.SemaphoreType.DMA((3,)),
            pltpu.SemaphoreType.DMA((3,)),
            pltpu.SemaphoreType.DMA((48,)),
            pltpu.SemaphoreType.DMA((48,)),
        ],
        compiler_params=pltpu.CompilerParams(
            collective_id=0, has_side_effects=True, vmem_limit_bytes=62 * 1024 * 1024
        ),
    )(
        tile_cols,
        tile_count,
        features.reshape(4, 128, 256),
        tile_vals,
        weight,
        bias.reshape(1, 256),
        cotangent,
    )
    act, wg, bg = pl.pallas_call(
        hand_over,
        out_shape=[jax.ShapeDtypeStruct(t.shape, t.dtype) for t in (act, wg, bg)],
        in_specs=[any_, any_, any_],
        out_specs=[any_, any_, any_],
        scratch_shapes=[pltpu.SemaphoreType.DMA((3,))],
        compiler_params=pltpu.CompilerParams(vmem_limit_bytes=62 * 1024 * 1024),
    )(act, wg, bg)
    return act, wg.reshape(256, 256), bg.reshape(256)


def solution(mesh):
    return jax.shard_map(
        body,
        mesh=mesh,
        in_specs=(
            P("blk", None),
            P("blk", None, "rep", None),
            P("blk", None),
            P("blk"),
            P(),
            P(),
            P(("blk", "rep"), None),
        ),
        out_specs=(P(("blk", "rep"), None), P(), P()),
        check_vma=False,
    )
```

time: 128 us -> 115 us (0.90)
  local copies, waits for them, and re-layouts: 8.19 us -> 0 us
  Pallas kernels: 119 us -> 115 us
    pallas_call x1, Pallas kernels: 119 us -> 103 us  [body(): pl.pallas_call(kernel, out_shape=[jax.ShapeDtypeStruct((128, 256), bf16),...]
    pallas_call x0 -> x1, Pallas kernels: none -> 11.1 us  [body(): pl.pallas_call(hand_over, out_shape=[jax.ShapeDtypeStruct(t.shape, t.dtyp...]
    unnamed x17 -> x0, local copies, waits for them, and re-layouts: 8.19 us -> none
where the time goes in v2:
time: 115 us
  Pallas kernels  115 us (100%)
    pallas_call x1, Pallas kernels, body(): pl.pallas_call(kernel, out_shape=[jax.ShapeDtypeStruct((128, 256), bf16),...  103 us
    pallas_call x1, Pallas kernels, body(): pl.pallas_call(hand_over, out_shape=[jax.ShapeDtypeStruct(t.shape, t.dtyp...  11.1 us

profile of v2, /device:TPU:1, one launch (start us, length us, event | category | flops | bytes accessed | tf_op | source)
XLA Modules:
  0.0 115.2 jit_solution(10679658534578453345)
XLA Ops:
  0.6 103.5 %shard_map.94 = (bf16[128,256]{1,0:T(8,128)(2,1)}, f32[32,8,256]{2,1,0:T(8,128)}, f32[1,256]{1,0:T(1,128)}) custom-call(s32[4,64]{1,0:T(4,128)} %cols.1, s32[4]{0:T(128)} %cnt.1, bf16[4,128,256]{2,1,0:T(8,128)(2,1)} %bitcast.4, bf16[4,64,32,128]{3,2,1,0:T(8,128)(2,1)} %vals.1, bf16[256,256]{1,0:T(8,128)(2,1)} %weight.1, f32[1,256]{1,0:T(1,128)} %bitcast.5, ...), custom_call_target="tpu_custom_call" | custom-call | tf_op jit(solution)/shard_map/pallas_call | solution.py:388
  104.1 11.1 %shard_map.95 = (bf16[128,256]{1,0:T(8,128)(2,1)}, f32[32,8,256]{2,1,0:T(8,128)}, f32[1,256]{1,0:T(1,128)}) custom-call(bf16[128,256]{1,0:T(8,128)(2,1)} %get-tuple-element.9.a, f32[32,8,256]{2,1,0:T(8,128)} %get-tuple-element.10.b, f32[1,256]{1,0:T(1,128)} %get-tuple-element.11.c), custom_call_target="tpu_custom_call" | custom-call | tf_op jit(solution)/shard_map/pallas_call | solution.py:443

commit v3 on v2

--- a/solution.py
+++ b/solution.py
@@ -12,8 +12,10 @@
 ZH = 8
 XY = 16
 Q = 64
-RELAYED = ((Q, 96), (Q + 96, 96))
+RELAYED = ((Q, 256 - Q),)
 PLAIN = ((-Q, 2 * Q),)
+CHUNKS = RELAYED + PLAIN
+SKIPS = (0, 2, 4, 6)
 STOP = 99
 
 
@@ -93,6 +95,8 @@
     across = b + 1 - 2 * xl
     sibling = r + 1 - 2 * core
     far = lax.rem(r + 2, 4)
+    up2 = lax.rem(b + 4, n_blk)
+    down2 = lax.rem(b + n_blk - 4, n_blk)
 
     def xy_dev(q):
         return dev((q % 4) * 64 + z * 2 + (q // 4) % 2, (q // 8) * 2 + core)
@@ -108,7 +112,7 @@
     )
     load_own.start()
     barrier = pltpu.get_barrier_semaphore()
-    partners = [dev(up, r), dev(down, r), dev(b, sibling)]
+    partners = [dev(up, r), dev(down, r), dev(b, sibling), dev(up2, r), dev(down2, r)]
     partners += [zl_dev(lax.rem(zl + u, ZL)) for u in range(1, ZL)]
     partners += [zh_dev(lax.rem(zh + u, ZH)) for u in range(1, ZH)]
     partners += [xy_dev(lax.rem(xy + u, XY)) for u in range(1, XY)]
@@ -125,7 +129,56 @@
 
     load_own.wait()
     win[8, 256:] = own[...].reshape(128, 256).T
-    win[16 * (1 - xl), : 256 - Q] = jnp.zeros((256 - Q, 128), jnp.bfloat16)
+    if Q < 256:
+        win[16 * (1 - xl), : 256 - Q] = jnp.zeros((256 - Q, 128), jnp.bfloat16)
+    pl.semaphore_wait(barrier, len(partners))
+
+    def chain(direction, src, dst, n):
+        sign = 2 * direction - 1
+        first, count = CHUNKS[n]
+        if isinstance(dst, int) and dst - src == 2:
+            to = up2 if direction == 0 else down2
+        else:
+            to = up if direction == 0 else down
+        return rcopy(
+            win.at[8 + sign * src, pl.ds(256 + first, count)],
+            win.at[8 + sign * dst, pl.ds(256 + first, count)],
+            hs.at[direction, n, dst - 1],
+            hr.at[direction, n, dst - 1],
+            dev(to, r),
+        )
+
+    def relay(off, n, sem):
+        first, count = RELAYED[n]
+        return rcopy(
+            win.at[off + 8, pl.ds(256 + first, count)],
+            win.at[off + 8, pl.ds(first - Q, count)],
+            xs.at[n, sem],
+            xr.at[n, sem],
+            dev(across, r),
+        )
+
+    n_rel = len(RELAYED)
+    n_all = n_rel + len(PLAIN)
+    swap = rcopy(
+        win.at[8, pl.ds(256, Q)], win.at[8, pl.ds(256 - Q, Q)], xs.at[0, 17], xr.at[0, 17], dev(across, r)
+    )
+    swap.start()
+    def children(k):
+        out = []
+        if k in SKIPS and k + 2 <= STEPS:
+            out.append(k + 2)
+        if k + 1 <= STEPS and k - 1 not in SKIPS:
+            out.append(k + 1)
+        return out
+
+    for n in range(n_all):
+        if CHUNKS[n][0] >= 0:
+            for dst in children(0):
+                chain(0, 0, dst, n).start()
+                chain(1, 0, dst, n).start()
+        if n < n_rel:
+            relay(0, n, 8).start()
     for j in range(4):
         vv[j, 64] = jnp.zeros((32, 128), jnp.bfloat16)
     acc[...] = jnp.zeros_like(acc)
@@ -147,44 +200,12 @@
         where_v[j : j + 1] = found[j]
     note = pltpu.make_async_copy(where_v, where_s, load_sem.at[5])
     note.start()
-    pl.semaphore_wait(barrier, len(partners))
-
-    def chain(direction, k, n):
-        off = -k if direction == 0 else k
-        to = off - 1 if direction == 0 else off + 1
-        first, count = (RELAYED + PLAIN)[n]
-        return rcopy(
-            win.at[off + 8, pl.ds(256 + first, count)],
-            win.at[to + 8, pl.ds(256 + first, count)],
-            hs.at[direction, n, k],
-            hr.at[direction, n, k],
-            dev(up if direction == 0 else down, r),
-        )
-
-    def relay(off, n, sem):
-        first, count = RELAYED[n]
-        return rcopy(
-            win.at[off + 8, pl.ds(256 + first, count)],
-            win.at[off + 8, pl.ds(first - Q, count)],
-            xs.at[n, sem],
-            xr.at[n, sem],
-            dev(across, r),
-        )
-
-    n_rel = len(RELAYED)
-    n_all = n_rel + len(PLAIN)
-    swap = rcopy(
-        win.at[8, pl.ds(256, Q)], win.at[8, pl.ds(256 - Q, Q)], xs.at[0, 17], xr.at[0, 17], dev(across, r)
-    )
-    swap.start()
-    for n in range(n_rel):
-        chain(0, 0, n).start()
-        chain(1, 0, n).start()
-        relay(0, n, 8).start()
     swap.wait_recv()
-    for n in range(n_rel, n_all):
-        chain(0, 0, n).start()
-        chain(1, 0, n).start()
+    for n in range(n_all):
+        if CHUNKS[n][0] < 0:
+            for dst in children(0):
+                chain(0, 0, dst, n).start()
+                chain(1, 0, dst, n).start()
     for c in loads:
         c.wait()
     note.wait()
@@ -193,9 +214,12 @@
         left = []
         for at in places:
             left.append(win[at, 256:])
-            left.append(jnp.concatenate([win[at, 256 - Q : 256], win[at, : 256 - Q]], axis=0))
+            if Q < 256:
+                left.append(jnp.concatenate([win[at, 256 - Q : 256], win[at, : 256 - Q]], axis=0))
+            else:
+                left.append(win[at, :256])
         left = jnp.concatenate(left, axis=1)
-        for pair in (0, 1):
+        for pair in (1 - xh, xh) if len(places) > 1 else (0, 1):
             right = []
             for j in (2 * pair, 2 * pair + 1):
                 tiles = [vv[j, where_s[j, at * 8 + u]] for at in places for u in range(8)]
@@ -212,37 +236,47 @@
             relay(-k, n, 8 - k).wait_recv()
             relay(k, n, 8 + k).wait_recv()
 
-    def step(k, _):
-        for n in range(n_rel):
+    def arrivals(k, dsts):
+        for n in range(n_all):
             for direction in (0, 1):
-                off = -k if direction == 0 else k
-                chain(direction, k - 1, n).wait_recv()
-                chain(direction, k, n).start()
-                relay(off, n, 8 + off).start()
-        for n in range(n_rel, n_all):
-            for direction in (0, 1):
-                chain(direction, k - 1, n).wait_recv()
-                chain(direction, k, n).start()
-
-        @pl.when(k > 1)
-        def _():
-            relays_in(k - 1)
-            for _ in products([8 - (k - 1)]):
-                pass
-            for _ in products([8 + (k - 1)]):
-                pass
-
-        return 0
+                chain(direction, k - 1, k, n).wait_recv()
+                for dst in dsts:
+                    chain(direction, k, dst, n).start()
+                if n < n_rel:
+                    off = -k if direction == 0 else k
+                    relay(off, n, 8 + off).start()
+
+    def multiply(k):
+        relays_in(k)
+        for _ in products([8 - k]):
+            pass
+        for _ in products([8 + k]):
+            pass
 
     for n in range(n_rel):
         relay(0, n, 8).wait_recv()
     for _ in products([8]):
         pass
-    lax.fori_loop(1, STEPS, step, 0)
+    tail = max(SKIPS + (-1,)) + 2
+    for k in range(1, tail):
+        arrivals(k, children(k))
+        if k > 1:
+            multiply(k - 1)
+
+    def step(k, _):
+        arrivals(k, [k + 1])
+
+        @pl.when(k > 1)
+        def _():
+            multiply(k - 1)
+
+        return 0
+
+    lax.fori_loop(tail, STEPS, step, 0)
     lasts = []
     for n in range(n_rel):
         for direction in (0, 1):
-            chain(direction, STEPS - 1, n).wait_recv()
+            chain(direction, STEPS - 1, STEPS, n).wait_recv()
         lasts.append(relay(8 - 16 * xl, n, 0))
         lasts[-1].start()
     relays_in(STEPS - 1)
@@ -252,29 +286,28 @@
         pass
     for n in range(n_rel, n_all):
         for direction in (0, 1):
-            chain(direction, STEPS - 1, n).wait_recv()
+            chain(direction, STEPS - 1, STEPS, n).wait_recv()
     for c in lasts:
         c.wait_recv()
     to_sibling = []
-    for pair in products([0, 16]):
-        c = rcopy(acc.at[2 * pair + 1 - core], got1.at[pair], ps.at[pair], pr.at[pair], dev(b, sibling))
+    for n, pair in enumerate(products([0, 16])):
+        c = rcopy(acc.at[2 * pair + 1 - core], got1.at[n], ps.at[n], pr.at[n], dev(b, sibling))
         c.start()
         to_sibling.append(c)
-    other = 1 - xh
     to_sibling[0].wait_recv()
-    to_sibling[1].wait_recv()
-    mine[...] = acc[2 * other + core] + got1[other]
+    mine[...] = acc[2 * (1 - xh) + core] + got1[0]
     c = rcopy(mine, got2, ps.at[2], pr.at[2], dev(b, far))
     c.start()
-    kept = acc[2 * xh + core] + got1[xh]
+    to_sibling[1].wait_recv()
+    kept = acc[2 * xh + core] + got1[1]
 
     def sent(k, _):
         for direction in (0, 1):
             for n in range(n_all):
-                chain(direction, k, n).wait_send()
+                chain(direction, k - 1, k, n).wait_send()
         return 0
 
-    lax.fori_loop(0, STEPS, sent, 0)
+    lax.fori_loop(1, STEPS + 1, sent, 0)
 
     def relay_sent(k, _):
         for n in range(n_rel):
@@ -369,16 +402,10 @@
     store_full.wait()
 
 
-def hand_over(a, b, c, a_out, b_out, c_out, sem):
-    copies = [
-        pltpu.make_async_copy(a, a_out, sem.at[0]),
-        pltpu.make_async_copy(b, b_out, sem.at[1]),
-        pltpu.make_async_copy(c, c_out, sem.at[2]),
-    ]
-    for d in copies:
-        d.start()
-    for d in copies:
-        d.wait()
+def hand_over(a, b, c, a_out, b_out, c_out):
+    a_out[...] = a[...]
+    b_out[...] = b[...]
+    c_out[...] = c[...]
 
 
 def body(features, tile_vals, tile_cols, tile_count, weight, bias, cotangent):
@@ -419,10 +446,10 @@
             pltpu.VMEM((32, 8, 256), f32),
             pltpu.VMEM((1, 256), f32),
             pltpu.SemaphoreType.DMA((6,)),
-            pltpu.SemaphoreType.DMA((2, len(RELAYED + PLAIN), STEPS)),
-            pltpu.SemaphoreType.DMA((2, len(RELAYED + PLAIN), STEPS)),
-            pltpu.SemaphoreType.DMA((len(RELAYED), 18)),
-            pltpu.SemaphoreType.DMA((len(RELAYED), 18)),
+            pltpu.SemaphoreType.DMA((2, len(CHUNKS), STEPS)),
+            pltpu.SemaphoreType.DMA((2, len(CHUNKS), STEPS)),
+            pltpu.SemaphoreType.DMA((max(len(RELAYED), 1), 18)),
+            pltpu.SemaphoreType.DMA((max(len(RELAYED), 1), 18)),
             pltpu.SemaphoreType.DMA((3,)),
             pltpu.SemaphoreType.DMA((3,)),
             pltpu.SemaphoreType.DMA((48,)),
@@ -443,9 +470,6 @@
     act, wg, bg = pl.pallas_call(
         hand_over,
         out_shape=[jax.ShapeDtypeStruct(t.shape, t.dtype) for t in (act, wg, bg)],
-        in_specs=[any_, any_, any_],
-        out_specs=[any_, any_, any_],
-        scratch_shapes=[pltpu.SemaphoreType.DMA((3,))],
         compiler_params=pltpu.CompilerParams(vmem_limit_bytes=62 * 1024 * 1024),
     )(act, wg, bg)
     return act, wg.reshape(256, 256), bg.reshape(256)

time: 115 us -> 105 us (0.913)
  Pallas kernels: 115 us -> 104 us
    pallas_call x1, Pallas kernels: 11.1 us -> 1.69 us  [body(): pl.pallas_call(hand_over, out_shape=[jax.ShapeDtypeStruct(t.shape, t.dtyp...]
where the time goes in v3:
time: 105 us
  Pallas kernels  104 us (99%)
    pallas_call x1, Pallas kernels, body(): pl.pallas_call(kernel, out_shape=[jax.ShapeDtypeStruct((128, 256), bf16),...  103 us

profile of v3, /device:TPU:1, one launch (start us, length us, event | category | flops | bytes accessed | tf_op | source)
XLA Modules:
  0.0 104.8 jit_solution(15531683218631611713)
XLA Ops:
  0.6 102.5 %shard_map.94 = (bf16[128,256]{1,0:T(8,128)(2,1)}, f32[32,8,256]{2,1,0:T(8,128)}, f32[1,256]{1,0:T(1,128)}) custom-call(s32[4,64]{1,0:T(4,128)} %cols.1, s32[4]{0:T(128)} %cnt.1, bf16[4,128,256]{2,1,0:T(8,128)(2,1)} %bitcast.4, bf16[4,64,32,128]{3,2,1,0:T(8,128)(2,1)} %vals.1, bf16[256,256]{1,0:T(8,128)(2,1)} %weight.1, f32[1,256]{1,0:T(1,128)} %bitcast.5, ...), custom_call_target="tpu_custom_call" | custom-call | tf_op jit(solution)/shard_map/pallas_call | solution.py:415
  103.2 1.7 %shard_map.95 = (bf16[128,256]{1,0:T(8,128)(2,1)}, f32[32,8,256]{2,1,0:T(8,128)}, f32[1,256]{1,0:T(1,128)}) custom-call(bf16[128,256]{1,0:T(8,128)(2,1)} %get-tuple-element.9.a, f32[32,8,256]{2,1,0:T(8,128)} %get-tuple-element.10.b, f32[1,256]{1,0:T(1,128)} %get-tuple-element.11.c), custom_call_target="tpu_custom_call" | custom-call | tf_op jit(solution)/shard_map/pallas_call | solution.py:470

commit v4 on v3

--- a/solution.py
+++ b/solution.py
@@ -11,12 +11,11 @@
 ZL = 4
 ZH = 8
 XY = 16
-Q = 64
+Q = 32
 RELAYED = ((Q, 256 - Q),)
 PLAIN = ((-Q, 2 * Q),)
 CHUNKS = RELAYED + PLAIN
 SKIPS = (0, 2, 4, 6)
-STOP = 99
 
 
 def dev(b, r):
@@ -347,6 +346,9 @@
             c = rcopy(src(p), dst, as_.at[base + u], ar.at[base + u], dev_of(p))
             c.start()
             copies.append(c)
+        for c in pending:
+            c.wait_send()
+        pending.clear()
         for c in copies:
             c.wait_recv()
         pending.extend(copies)
@@ -392,11 +394,11 @@
     half = full.at[pl.ds(core * XY, XY)]
     c = rcopy(half, half, as_.at[32], ar.at[32], dev(b, sibling))
     c.start()
+    for d in pending:
+        d.wait_send()
     c.wait()
     store_full = pltpu.make_async_copy(full, wg_out, load_sem.at[2])
     store_full.start()
-    for c in pending:
-        c.wait_send()
     store_act.wait()
     store_bias.wait()
     store_full.wait()

time: 105 us -> 104 us (level)
  no operation moved by 1% of the time
where the time goes in v4:
time: 104 us
  Pallas kernels  103 us (99%)
    pallas_call x1, Pallas kernels, body(): pl.pallas_call(kernel, out_shape=[jax.ShapeDtypeStruct((128, 256), bf16),...  102 us

profile of v4, /device:TPU:1, one launch (start us, length us, event | category | flops | bytes accessed | tf_op | source)
XLA Modules:
  0.0 104.1 jit_solution(4043345085910583866)
XLA Ops:
  0.6 101.8 %shard_map.94 = (bf16[128,256]{1,0:T(8,128)(2,1)}, f32[32,8,256]{2,1,0:T(8,128)}, f32[1,256]{1,0:T(1,128)}) custom-call(s32[4,64]{1,0:T(4,128)} %cols.1, s32[4]{0:T(128)} %cnt.1, bf16[4,128,256]{2,1,0:T(8,128)(2,1)} %bitcast.4, bf16[4,64,32,128]{3,2,1,0:T(8,128)(2,1)} %vals.1, bf16[256,256]{1,0:T(8,128)(2,1)} %weight.1, f32[1,256]{1,0:T(1,128)} %bitcast.5, ...), custom_call_target="tpu_custom_call" | custom-call | tf_op jit(solution)/shard_map/pallas_call | solution.py:417
  102.4 1.7 %shard_map.95 = (bf16[128,256]{1,0:T(8,128)(2,1)}, f32[32,8,256]{2,1,0:T(8,128)}, f32[1,256]{1,0:T(1,128)}) custom-call(bf16[128,256]{1,0:T(8,128)(2,1)} %get-tuple-element.9.a, f32[32,8,256]{2,1,0:T(8,128)} %get-tuple-element.10.b, f32[1,256]{1,0:T(1,128)} %get-tuple-element.11.c), custom_call_target="tpu_custom_call" | custom-call | tf_op jit(solution)/shard_map/pallas_call | solution.py:472
